TPU v7x, 32 devices: a whole 2x2x4 slice. The times are simulated.
32 devices in a mesh: dp: 16 (over z, y, x), fsdp: 2 (over core).
Axes of the slice: x: 2, y: 2, z: 4, core: 2. Of those that a mesh axis runs over, the one named last changes fastest.
Arguments:
- teacher_feat: bfloat16 [1024, 256], P(('dp', 'fsdp')), may hold values from -1 to 1
- student_feat: bfloat16 [1024, 256], P(('dp', 'fsdp')), may hold values from -1 to 1
- crop_weight: bfloat16 [1024], P(('dp', 'fsdp')), may hold values from -96 to 96
- teacher_v: bfloat16 [256, 32768], P(None, 'fsdp'), may hold values from -2 to 2
- student_v: bfloat16 [256, 32768], P(None, 'fsdp'), may hold values from -2 to 2
Outputs:
- grad_v: float32 [256, 32768], P('dp', 'fsdp')
- grad_feat: float32 [1024, 256], P(('dp', 'fsdp'))
All inputs are finite; a program needn't handle non-finite values.
Results may differ from a plain program's by a relative error of at most 0.0073.
Values may be sent and summed in bfloat16 or wider, within the bound.
No kernel may reach another device: no remote copies, remote signals or barrier semaphores. Data moves between devices by JAX's collectives and lax.ppermute only.
A program may use at most 128 MiB of HBM per device.

v0:
```python
import jax
import jax.numpy as jnp
from jax import lax
from jax.sharding import PartitionSpec as P

K = 32768
ITERS = 3


teacher_temp = 0.04
student_temp = 0.1
epsilon = 1e-06


def unit_rows(values):
    floats = values.astype(jnp.float32)
    length = jnp.sqrt(jnp.sum(floats * floats, axis=1, keepdims=True) + epsilon)
    return (floats / length, length)


def unit_columns(values):
    floats = values.astype(jnp.float32)
    length = jnp.sqrt(jnp.sum(floats * floats, axis=0, keepdims=True) + epsilon)
    return (floats / length, length)


def scale_prototypes(mass):
    proto_mass = lax.psum(jnp.sum(mass, axis=0), "dp")
    return mass / (proto_mass * K)[None, :]


def scale_crops(mass, crop_count):
    crop_mass = lax.psum(jnp.sum(mass, axis=1), "fsdp")
    return mass / (crop_mass * crop_count)[:, None]


def body(teacher_feat, student_feat, crop_weight, teacher_v, student_v):
    teacher_rows, student_rows, weight_rows = (
        lax.all_gather(teacher_feat, "fsdp", axis=0, tiled=True),
        lax.all_gather(student_feat, "fsdp", axis=0, tiled=True),
        lax.all_gather(crop_weight, "fsdp", axis=0, tiled=True),
    )
    local_rows = teacher_feat.shape[0]
    crop_count = teacher_rows.shape[0] * lax.axis_size("dp")
    teacher_hat, _ = unit_rows(teacher_rows)
    student_hat, student_len = unit_rows(student_rows)
    teacher_w, _ = unit_columns(teacher_v)
    student_w, student_wlen = unit_columns(student_v)
    student_unit = student_hat.astype(jnp.bfloat16)
    student_wunit = student_w.astype(jnp.bfloat16)
    teacher_mass = jnp.exp(
        jnp.dot(
            teacher_hat.astype(jnp.bfloat16),
            teacher_w.astype(jnp.bfloat16),
            preferred_element_type=jnp.float32,
        )
        / teacher_temp
    )
    student_mass = jnp.exp(
        jnp.dot(student_unit, student_wunit, preferred_element_type=jnp.float32) / student_temp
    )
    student_part = jnp.sum(student_mass, axis=1)
    student_total = lax.psum(student_part, "fsdp")
    first_sweep = 0
    for sweep_index in range(first_sweep, ITERS):
        teacher_mass = scale_prototypes(teacher_mass)
        teacher_mass = scale_crops(teacher_mass, crop_count)
    target = teacher_mass * crop_count
    student_prob = student_mass / student_total[:, None]
    gradient = (
        (student_prob - target) * weight_rows.astype(jnp.float32)[:, None] / student_temp
    ).astype(jnp.bfloat16)
    feature_part = lax.dot_general(
        gradient, student_wunit, (((1,), (1,)), ((), ())), preferred_element_type=jnp.float32
    )
    feature_grad = lax.psum(feature_part, "fsdp")
    first_row = lax.axis_index("fsdp") * local_rows
    own_grad = lax.dynamic_slice_in_dim(feature_grad, first_row, local_rows, 0)
    own_hat = lax.dynamic_slice_in_dim(student_hat, first_row, local_rows, 0)
    own_len = lax.dynamic_slice_in_dim(student_len, first_row, local_rows, 0)
    grad_feat = (own_grad - own_hat * jnp.sum(own_hat * own_grad, axis=1, keepdims=True)) / own_len
    weight_part = lax.dot_general(
        student_unit, gradient, (((0,), (0,)), ((), ())), preferred_element_type=jnp.float32
    )
    weight_grad = lax.psum_scatter(weight_part, "dp", scatter_dimension=0, tiled=True)
    slab_rows = weight_grad.shape[0]
    unit_slab = lax.dynamic_slice_in_dim(student_w, lax.axis_index("dp") * slab_rows, slab_rows, 0)
    weight_dot = lax.psum(jnp.sum(unit_slab * weight_grad, axis=0), "dp")
    grad_v = (weight_grad - unit_slab * weight_dot[None, :]) / student_wlen
    return (grad_v, grad_feat)


def solution(mesh):
    placed = (
        P(("dp", "fsdp"), None),
        P(("dp", "fsdp"), None),
        P(("dp", "fsdp")),
        P(None, "fsdp"),
        P(None, "fsdp"),
    )
    return jax.shard_map(
        body,
        mesh=mesh,
        in_specs=placed,
        out_specs=(P("dp", "fsdp"), P(("dp", "fsdp"), None)),
        check_vma=False,
    )
```

profile of v0, /device:TPU:0, one launch (start us, length us, event | category | flops | bytes accessed | tf_op | source)
XLA Modules:
  0.0 853.9 jit_solution(3450498279505954982)
XLA Ops:
  7.2 0.0 all-reduce.8.cloned.1.call-start
  7.2 2.2 all_gather.10
  9.4 0.1 fusion.23
  9.5 0.0 copy-start
  9.5 5.3 fusion.3
  14.8 0.5 copy-done
  15.3 0.0 copy-start.1
  15.3 4.7 fusion.30
  19.9 0.0 all-reduce.8.cloned.1.call-update
  20.0 0.0 all-reduce.10.cloned.1.call-start
  20.0 0.0 copy-done.1
  20.0 1.8 all_gather.9
  21.8 5.1 fusion.2
  27.0 0.1 fusion.22
  27.1 97.6 %all-reduce.8.cloned.1.call-done = f32[16384]{0:T(1024)} async-done(((f32[16384]{0:T(1024)}), f32[16384]{0:T(1024)}) %all-reduce.8.cloned.1.call-update) | async-done | bytes 65552 | tf_op jit(solution)/shard_map/psum | solution.py:28
  124.7 0.8 broadcast_multiply_fusion.2
  125.5 2.6 divide_reduce_fusion
  128.1 2.5 psum.65
  130.6 3.7 fusion.18
  134.3 0.0 all-reduce.10.cloned.1.call-update
  134.3 0.0 all-reduce.12.cloned.1.call-start
  134.3 101.1 %all-reduce.10.cloned.1.call-done = f32[16384]{0:T(1024)} async-done(((f32[16384]{0:T(1024)}), f32[16384]{0:T(1024)}) %all-reduce.10.cloned.1.call-update) | async-done | bytes 65552 | tf_op jit(solution)/shard_map/psum | solution.py:28
  235.4 0.8 broadcast_multiply_fusion.1
  236.3 3.0 fusion.19
  239.3 2.5 psum.67
  241.8 3.8 fusion.20
  245.6 0.0 all-reduce.12.cloned.1.call-update
  245.6 0.0 copy-start.3
  245.6 0.0 copy-start.2
  245.6 0.0 all-reduce.16.cloned.1.call-start
  245.7 7.9 fusion.31
  253.6 0.0 copy-done.3
  253.6 0.6 dynamic-slice.4
  254.8 0.0 copy-done.2
  254.9 0.2 dynamic-update-slice
  255.1 2.6 all-reduce
  257.7 89.1 %all-reduce.12.cloned.1.call-done = f32[16384]{0:T(1024)} async-done(((f32[16384]{0:T(1024)}), f32[16384]{0:T(1024)}) %all-reduce.12.cloned.1.call-update) | async-done | bytes 65552 | tf_op jit(solution)/shard_map/psum | solution.py:28
  346.8 0.8 broadcast_multiply_fusion
  347.7 3.3 fusion.21
  351.0 2.5 all-reduce.1
  353.5 9.7 %fusion.15 = f32[64,256]{1,0:T(8,128)} fusion(bf16[256,16384]{1,0:T(8,128)(2,1)} %param.9, f32[16384]{0:T(1024)S(1)} %add_sqrt_fusion.1, f32[64,16384]{1,0:T(8,128)} %get-tuple-element.5, f32[64,16384]{1,0:T(8,128)} %get-tuple-element.7, f32[64]{0:T(128)S(1)} %convert_element_type.38, f32[64]{0:T(128)S(1)} %broadcast_multiply_fusion.3, ...), kind=kOutput, calls=%fused_computation.23 | convolution fusion | flops 562036736 | bytes 17106176 | tf_op jit(solution)/shard_map/dot_general | solution.py:73
  363.2 0.0 all-reduce.16.cloned.1.call-update
  363.2 0.0 reduce-scatter.2.cloned.1.call-start
  363.3 11.7 %fusion.27 = f32[256,16384]{1,0:T(8,128)} fusion(bf16[64,256]{1,0:T(8,128)(2,1)S(1)} %all_gather.9, f32[64]{0:T(128)S(1)} %add_sqrt_fusion.3, f32[64,16384]{1,0:T(8,128)} %get-tuple-element.5, f32[64,16384]{1,0:T(8,128)} %get-tuple-element.7, f32[64]{0:T(128)S(1)} %convert_element_type.38, f32[64]{0:T(128)S(1)} %broadcast_multiply_fusion.3, ...), kind=kOutput, calls=%fused_computation.48 | convolution fusion | flops 549502976 | bytes 25396736 | tf_op jit(solution)/shard_map/dot_general | solution.py:82
  374.9 0.0 reduce-scatter.2.cloned.1.call-update
  374.9 0.0 all-reduce.14.cloned.1.call-start
  375.0 0.1 dynamic-slice.3
  375.1 0.1 convert_divide_fusion.3
  375.2 11.3 %convert_divide_fusion.1 = f32[256,16384]{1,0:T(8,128)} fusion(bf16[256,16384]{1,0:T(8,128)(2,1)} %param.9, f32[16384]{0:T(1024)S(1)} %add_sqrt_fusion.1), kind=kLoop, calls=%fused_computation.2 | loop fusion | flops 8388608 | bytes 25231360 | tf_op jit(solution)/shard_map/div | solution.py:24
  386.4 0.0 all-reduce.16.cloned.1.call-done
  386.4 0.9 multiply_reduce_fusion.1
  387.3 342.7 %reduce-scatter.2.cloned.1.call-done = f32[16,16384]{1,0:T(8,128)} async-done(((f32[256,16384]{1,0:T(8,128)}), f32[16,16384]{1,0:T(8,128)}) %reduce-scatter.2.cloned.1.call-update) | async-done | bytes 1048592 | tf_op jit(solution)/shard_map/reduce_scatter | solution.py:85
  730.0 2.4 multiply_reduce_fusion
  732.3 0.0 all-reduce.14.cloned.1.call-update
  732.4 1.5 subtract_divide_fusion.1
  733.8 110.5 %all-reduce.14.cloned.1.call-done = f32[16384]{0:T(1024)} async-done(((f32[16384]{0:T(1024)}), f32[16384]{0:T(1024)}) %all-reduce.14.cloned.1.call-update) | async-done | bytes 65552 | tf_op jit(solution)/shard_map/psum | solution.py:88
  844.4 2.7 subtract_divide_fusion
  (9 shorter events, 0.1 us)
Async XLA Ops:
  7.2 117.5 %all-reduce.8.cloned.1.call-start = ((), (), s32[]{:S(2)}) async-start(), calls=%async_computation.1 | async-start | bytes 131072 | tf_op jit(solution)/shard_map/psum | solution.py:28
  9.5 5.8 copy-start
  15.3 4.7 copy-start.1
  20.0 215.5 %all-reduce.10.cloned.1.call-start = ((), (), s32[]{:S(2)}) async-start(), calls=%async_computation.2 | async-start | bytes 131072 | tf_op jit(solution)/shard_map/psum | solution.py:28
  134.3 212.6 %all-reduce.12.cloned.1.call-start = ((), (), s32[]{:S(2)}) async-start(), calls=%async_computation.3 | async-start | bytes 131072 | tf_op jit(solution)/shard_map/psum | solution.py:28
  245.6 8.0 copy-start.3
  245.6 9.2 %copy-start.2 = (bf16[32]{0:T(256)(128)(2,1)S(1)}, bf16[32]{0:T(256)(128)(2,1)}, u32[]{:S(2)}) copy-start(bf16[32]{0:T(256)(128)(2,1)} %param.7) | copy-start | bytes 196
  245.6 140.8 %all-reduce.16.cloned.1.call-start = ((), (), s32[]{:S(2)}) async-start(), calls=%async_computation.6 | async-start | bytes 131072 | tf_op jit(solution)/shard_map/psum | solution.py:76
  363.2 366.8 %reduce-scatter.2.cloned.1.call-start = ((), (), s32[]{:S(2)}) async-start(), calls=%async_computation.4 | async-start | bytes 17825792 | tf_op jit(solution)/shard_map/reduce_scatter | solution.py:85
  374.9 469.4 %all-reduce.14.cloned.1.call-start = ((), (), s32[]{:S(2)}) async-start(), calls=%async_computation.5 | async-start | bytes 131072 | tf_op jit(solution)/shard_map/psum | solution.py:88
Sparse Core Ops, SparseCore 0:
  20.1 104.5 all-reduce.7
  134.4 100.9 all-reduce.9
  245.7 101.0 all-reduce.11
  363.3 16.7 all-reduce.15
  382.4 347.5 reduce-scatter.1
  736.8 107.5 all-reduce.13
where the time goes:
time: 855 us; the launch traced here: 854 us
  waiting for transfers between devices  741 us (87%)
  other arithmetic  48.3 us (6%)
  matrix products  33.9 us (4%)
  between operations  14.9 us (2%)
  blocking collectives  14 us (2%)
    reduce_scatter x1, waiting for transfers between devices, body(): lax.psum_scatter(weight_part, 'dp', scatter_dimension=0, tiled=True)  343 us
    psum x3, waiting for transfers between devices, scale_prototypes(): proto_mass = lax.psum(jnp.sum(mass, axis=0), 'dp')  288 us
    psum x1, waiting for transfers between devices, body(): weight_dot = lax.psum(jnp.sum(unit_slab * weight_grad, axis=0), 'dp')  111 us
  transfers between devices with their start and end apart: 6, of which 5 were waited for; matrix products, arithmetic and copies ran while one was open for 5% of the time, Pallas kernels for 0%

commit v1 on v0

v1 whole, which is shorter than its diff:
```python
import jax
import jax.numpy as jnp
from jax import lax
from jax.sharding import PartitionSpec as P

ITERS = 3

teacher_temp = 0.04
student_temp = 0.1
epsilon = 1e-06

EVERY = ("dp", "fsdp")


def unit_rows(values):
    floats = values.astype(jnp.float32)
    length = jnp.sqrt(jnp.sum(floats * floats, axis=1, keepdims=True) + epsilon)
    return (floats / length, length)


def unit_columns(values):
    floats = values.astype(jnp.float32)
    length = jnp.sqrt(jnp.sum(floats * floats, axis=0, keepdims=True) + epsilon)
    return (floats / length, length)


def body(teacher_feat, student_feat, crop_weight, teacher_v, student_v):
    devices = lax.axis_size("dp") * lax.axis_size("fsdp")
    own_rows, width = teacher_feat.shape
    crops = own_rows * devices
    block = teacher_v.shape[1] // lax.axis_size("dp")
    prototypes = block * devices
    first = lax.axis_index("dp") * block

    teacher_hat, _ = unit_rows(teacher_feat)
    student_hat, student_len = unit_rows(student_feat)
    units = jnp.concatenate(
        [teacher_hat.astype(jnp.bfloat16), student_hat.astype(jnp.bfloat16)], axis=1
    )
    units = lax.all_gather(units, EVERY, axis=0, tiled=True)
    teacher_unit, student_unit = units[:, :width], units[:, width:]
    weights = lax.all_gather(crop_weight, EVERY, axis=0, tiled=True).astype(jnp.float32)

    teacher_w, _ = unit_columns(lax.dynamic_slice_in_dim(teacher_v, first, block, 1))
    student_w, student_wlen = unit_columns(lax.dynamic_slice_in_dim(student_v, first, block, 1))
    student_wunit = student_w.astype(jnp.bfloat16)

    mass = jnp.exp(
        jnp.dot(teacher_unit, teacher_w.astype(jnp.bfloat16), preferred_element_type=jnp.float32)
        / teacher_temp
    )
    student_mass = jnp.exp(
        jnp.dot(student_unit, student_wunit, preferred_element_type=jnp.float32) / student_temp
    )
    student_part = jnp.sum(student_mass, axis=1)

    crop_scale = None
    for sweep in range(ITERS):
        scaled = mass if sweep == 0 else mass * crop_scale[:, None]
        proto_scale = 1.0 / (prototypes * jnp.sum(scaled, axis=0))
        crop_part = jnp.sum(mass * proto_scale[None, :], axis=1)
        if sweep == 0:
            sums = lax.psum(jnp.stack([crop_part, student_part]), EVERY)
            crop_mass, student_total = sums[0], sums[1]
        else:
            crop_mass = lax.psum(crop_part, EVERY)
        crop_scale = 1.0 / (crops * crop_mass)

    target = crops * (mass * crop_scale[:, None] * proto_scale[None, :])
    student_prob = student_mass / student_total[:, None]
    gradient = ((student_prob - target) * weights[:, None] / student_temp).astype(jnp.bfloat16)
    feature_part = lax.dot_general(
        gradient, student_wunit, (((1,), (1,)), ((), ())), preferred_element_type=jnp.float32
    )
    weight_grad = lax.dot_general(
        student_unit, gradient, (((0,), (0,)), ((), ())), preferred_element_type=jnp.float32
    )
    weight_dot = jnp.sum(student_w * weight_grad, axis=0, keepdims=True)
    grad_block = (weight_grad - student_w * weight_dot) / student_wlen

    feature_all = lax.all_to_all(
        feature_part.astype(jnp.bfloat16).reshape(devices, own_rows, width), EVERY, 0, 0
    )
    feature_grad = jnp.sum(feature_all.astype(jnp.float32), axis=0)
    grad_feat = (
        feature_grad - student_hat * jnp.sum(student_hat * feature_grad, axis=1, keepdims=True)
    ) / student_len
    grad_v = lax.all_to_all(grad_block.astype(jnp.bfloat16), "dp", 0, 1, tiled=True)
    return (grad_v.astype(jnp.float32), grad_feat)


def solution(mesh):
    placed = (
        P(EVERY, None),
        P(EVERY, None),
        P(EVERY),
        P(None, "fsdp"),
        P(None, "fsdp"),
    )
    return jax.shard_map(
        body,
        mesh=mesh,
        in_specs=placed,
        out_specs=(P("dp", "fsdp"), P(EVERY, None)),
        check_vma=False,
    )
```

time: 855 us -> 258 us (0.30)
  waiting for transfers between devices: 741 us -> 38.7 us
  blocking collectives: 14 us -> 162 us
  other arithmetic: 48.3 us -> 18.6 us
  matrix products: 33.9 us -> 10.4 us
    psum x5 -> x0, waiting for transfers between devices: 398 us -> none  [the longest x3 288 us: scale_prototypes(): proto_mass = lax.psum(jnp.sum(mass, axis=0), 'dp')]
    reduce_scatter x1 -> x0, waiting for transfers between devices: 343 us -> none  [body(): lax.psum_scatter(weight_part, 'dp', scatter_dimension=0, tiled=True)]
    psum x3, blocking collectives: 7.41 us -> 120 us  [the longest x2 80.2 us: body(): crop_mass = lax.psum(crop_part, EVERY)]
    unnamed x1, blocking collectives: 2.63 us -> 42 us
    all_to_all x0 -> x2, waiting for transfers between devices: none -> 25.6 us  [the longest x1 14.3 us: body(): lax.all_to_all(feature_part.astype(jnp.bfloat16).reshape(devices, own_row...]
    div x4 -> x6, other arithmetic: 15.5 us -> 0.73 us  [the longest x1 0.71 us: body(): (feature_grad - student_hat * jnp.sum(student_hat * feature_grad, axis=1,...]
    all_gather x0 -> x1, waiting for transfers between devices: none -> 13.1 us  [body(): units = lax.all_gather(units, EVERY, axis=0, tiled=True)]
    reduce_sum x7, other arithmetic: 19.6 us -> 6.67 us  [the longest x2 5.37 us: body(): proto_scale = 1.0 / (prototypes * jnp.sum(scaled, axis=0))]
  transfers between devices with their start and end apart: 6 -> 3, of which waited for: 5 -> 3; matrix products, arithmetic and copies ran while one was open for 5% -> 2% of each run, Pallas kernels for 0% -> 0%
where the time goes in v1:
time: 258 us; the launch traced here: 257 us
  blocking collectives  162 us (63%)
  waiting for transfers between devices  38.7 us (15%)
  other arithmetic  18.6 us (7%)
  between operations  14.2 us (6%)
  matrix products  10.4 us (4%)
  starting transfers between devices  7.97 us (3%)
  local copies, waits for them, and re-layouts  5.04 us (2%)
    psum x2, blocking collectives, body(): crop_mass = lax.psum(crop_part, EVERY)  80.2 us
    unnamed x1, blocking collectives  42 us
    psum x1, blocking collectives, body(): sums = lax.psum(jnp.stack([crop_part, student_part]), EVERY)  39.5 us
    all_to_all x1, waiting for transfers between devices, body(): lax.all_to_all(feature_part.astype(jnp.bfloat16).reshape(devices, own_row...  14.3 us
    all_gather x1, waiting for transfers between devices, body(): units = lax.all_gather(units, EVERY, axis=0, tiled=True)  13.1 us
    all_to_all x1, waiting for transfers between devices, body(): lax.all_to_all(grad_block.astype(jnp.bfloat16), 'dp', 0, 1, tiled=True)  11.3 us
    reduce_sum x2, other arithmetic, body(): proto_scale = 1.0 / (prototypes * jnp.sum(scaled, axis=0))  5.37 us
  transfers between devices with their start and end apart: 3, of which 3 were waited for; matrix products, arithmetic and copies ran while one was open for 2% of the time, Pallas kernels for 0%

profile of v1, /device:TPU:0, one launch (start us, length us, event | category | flops | bytes accessed | tf_op | source)
XLA Modules:
  0.0 256.7 jit_solution(8444640604660109290)
XLA Ops:
  7.2 0.0 all-gather.2.cloned.1.call-start
  7.2 0.8 fusion.14
  8.0 0.8 fusion.16
  8.9 0.8 fusion.15
  9.7 0.6 pad_maximum_fusion
  10.3 0.0 all-gather.2.cloned.1.call-update
  10.4 0.8 dynamic-update-slice
  11.2 42.0 %all-reduce = bf16[1024]{0:T(1024)(128)(2,1)S(1)} all-reduce(bf16[1024]{0:T(1024)(128)(2,1)S(1)} %dynamic-update-slice), channel_id=1, replica_groups=mesh['dp'=16,'fsdp'=2] {'dp','fsdp'}, use_global_device_ids=true, to_apply=%add | all-reduce | flops 1024 | bytes 4096
  53.3 1.4 fusion.1
  54.7 13.1 %all-gather.2.cloned.1.call-done = bf16[1024,512]{1,0:T(8,128)(2,1)} async-done(((bf16[32,512]{1,0:T(8,128)(2,1)}), bf16[1024,512]{1,0:T(8,128)(2,1)}) %all-gather.2.cloned.1.call-update) | async-done | bytes 1048592 | tf_op jit(solution)/shard_map/all_gather | solution.py:40
  67.8 2.1 fusion.21
  70.0 0.0 copy-start
  70.0 0.0 copy-start.4
  70.0 0.3 multiply_reduce_fusion.4
  70.4 1.6 copy-done.4
  72.0 3.8 %fusion = (f32[1024]{0:T(1024)S(1)}, f32[1024,1024]{0,1:T(8,128)}) fusion(f32[1024]{0:T(1024)S(1)} %add_sqrt_fusion.1, bf16[256,16384]{1,0:T(8,128)(2,1)} %param.9, s32[]{:T(128)S(6)} %select_n.4, bf16[1024,512]{1,0:T(8,128)(2,1)S(1)} %copy-done.4), kind=kOutput, calls=%fused_computation.8 | convolution fusion | flops 539753472 | bytes 5251076 | tf_op jit(solution)/shard_map/dot_general | solution.py:53
  75.8 0.0 copy-done
  75.8 39.5 %psum.21 = f32[2,1024]{1,0:T(2,128)S(1)} all-reduce(f32[2,1024]{1,0:T(2,128)S(1)} %pad_maximum_fusion.1), channel_id=1, replica_groups=mesh['dp'=16,'fsdp'=2] {'dp','fsdp'}, use_global_device_ids=true, to_apply=%region_7.0 | all-reduce | flops 2048 | bytes 16384 | tf_op jit(solution)/shard_map/psum | solution.py:63
  115.3 0.0 copy-start.1
  115.3 2.7 %multiply_reduce_fusion.3 = f32[1024]{0:T(1024)S(1)} fusion(f32[1024,1024]{0,1:T(8,128)} %copy-done, f32[1024]{0:T(1024)S(1)} %bitcast.15), kind=kLoop, calls=%fused_computation.4 | loop fusion | flops 2096128 | bytes 4202496 | tf_op jit(solution)/shard_map/reduce_sum | solution.py:60
  118.0 0.7 copy-done.1
  118.8 0.3 multiply_reduce_fusion.2
  119.1 39.9 %psum.22 = f32[1024]{0:T(1024)S(1)} all-reduce(f32[1024]{0:T(1024)S(1)} %multiply_reduce_fusion.2), channel_id=1, replica_groups=mesh['dp'=16,'fsdp'=2] {'dp','fsdp'}, use_global_device_ids=true, to_apply=%region_10.0 | all-reduce | flops 1024 | bytes 8192 | tf_op jit(solution)/shard_map/psum | solution.py:66
  159.0 0.0 copy-start.2
  159.0 2.7 %multiply_reduce_fusion.1 = f32[1024]{0:T(1024)S(1)} fusion(f32[1024,1024]{0,1:T(8,128)} %copy-done, f32[1024]{0:T(1024)S(1)} %multiply_divide_fusion.2), kind=kLoop, calls=%fused_computation.2 | loop fusion | flops 2096128 | bytes 4202496 | tf_op jit(solution)/shard_map/reduce_sum | solution.py:60
  161.7 0.7 copy-done.2
  162.4 0.3 multiply_reduce_fusion
  162.8 40.3 %psum.23 = f32[1024]{0:T(1024)S(1)} all-reduce(f32[1024]{0:T(1024)S(1)} %multiply_reduce_fusion), channel_id=1, replica_groups=mesh['dp'=16,'fsdp'=2] {'dp','fsdp'}, use_global_device_ids=true, to_apply=%region_13.0 | all-reduce | flops 1024 | bytes 8192 | tf_op jit(solution)/shard_map/psum | solution.py:66
  203.1 0.0 copy-start.5
  203.1 4.4 %multiply_convert_fusion = bf16[1024,1024]{0,1:T(8,128)(2,1)S(1)} fusion(f32[1024,1024]{0,1:T(8,128)} %copy-done, f32[1024,1024]{0,1:T(8,128)} %get-tuple-element.5, f32[1024]{0:T(1024)S(1)} %convert_element_type.56, f32[1024]{0:T(1024)S(1)} %multiply_divide_fusion, f32[1024]{0:T(1024)S(1)} %multiply_divide_fusion.1, f32[1024]{0:T(1024)S(1)} %bitcast.13), kind=kLoop, calls=%fused_computation | loop fusion | flops 9437184 | bytes 10502144 | tf_op jit(solution)/shard_map/convert_element_type | solution.py:71
  207.5 0.0 copy-done.5
  207.5 1.8 multiply_reduce_fusion.5
  209.4 2.1 divide_convert_fusion
  211.5 5.1 %all-to-all-start = ((bf16[16,16,1024]{2,1,0:T(8,128)(2,1)}), bf16[16,16,1024]{2,1,0:T(8,128)(2,1)S(1)}, u32[]{:S(2)}, u32[]{:S(2)}) async-start(bf16[16,16,1024]{2,1,0:T(8,128)(2,1)} %bitcast.4), calls=%async_computation | async-start | bytes 1048576 | tf_op jit(solution)/shard_map/all_to_all | solution.py:88
  216.6 2.6 %convolution_convert_fusion = bf16[1024,256]{1,0:T(8,128)(2,1)} fusion(bf16[1024,1024]{0,1:T(8,128)(2,1)S(1)} %multiply_convert_fusion, f32[1024]{0:T(1024)S(1)} %add_sqrt_fusion.1, bf16[256,16384]{1,0:T(8,128)(2,1)} %param.9, s32[]{:T(128)S(6)} %select_n.4), kind=kOutput, calls=%fused_computation.13 | convolution fusion | flops 537919488 | bytes 3149828 | tf_op jit(solution)/shard_map/dot_general | solution.py:72
  219.2 0.0 copy-start.3
  219.2 11.3 %all-to-all-done = bf16[16,16,1024]{2,1,0:T(8,128)(2,1)S(1)} async-done(((bf16[16,16,1024]{2,1,0:T(8,128)(2,1)}), bf16[16,16,1024]{2,1,0:T(8,128)(2,1)S(1)}, u32[]{:S(2)}, u32[]{:S(2)}) %all-to-all-start) | async-done | bytes 524320 | tf_op jit(solution)/shard_map/all_to_all | solution.py:88
  230.4 2.8 %all-to-all-start.1 = ((bf16[32,32,256]{2,1,0:T(8,128)(2,1)}), bf16[32,32,256]{2,1,0:T(8,128)(2,1)S(1)}, u32[]{:S(2)}, u32[]{:S(2)}) async-start(bf16[32,32,256]{2,1,0:T(8,128)(2,1)} %bitcast.6), calls=%async_computation.1 | async-start | bytes 1048576 | tf_op jit(solution)/shard_map/all_to_all | solution.py:81
  233.3 0.1 convert_bitcast_fusion
  233.4 1.1 copy.10
  234.5 14.3 %all-to-all-done.1 = bf16[32,32,256]{2,1,0:T(8,128)(2,1)S(1)} async-done(((bf16[32,32,256]{2,1,0:T(8,128)(2,1)}), bf16[32,32,256]{2,1,0:T(8,128)(2,1)S(1)}, u32[]{:S(2)}, u32[]{:S(2)}) %all-to-all-start.1) | async-done | bytes 524320 | tf_op jit(solution)/shard_map/all_to_all | solution.py:81
  248.8 0.1 convert_reduce_fusion
  248.9 0.0 copy-done.3
  248.9 0.2 multiply_reduce_fusion.6
  249.1 0.7 subtract_divide_fusion
  (13 shorter events, 0.1 us)
Async XLA Ops:
  7.2 60.7 %all-gather.2.cloned.1.call-start = ((), (), s32[]{:S(2)}) async-start(), calls=%async_computation.2 | async-start | bytes 1081344 | tf_op jit(solution)/shard_map/all_gather | solution.py:40
  70.0 5.8 %copy-start = (f32[1024,1024]{0,1:T(8,128)}, f32[1024,1024]{0,1:T(8,128)S(1)}, u32[]{:S(2)}) copy-start(f32[1024,1024]{0,1:T(8,128)S(1)} %get-tuple-element.7) | copy-start | bytes 12582916
  70.0 2.0 copy-start.4
  115.3 3.4 %copy-start.1 = (f32[1024,1024]{0,1:T(8,128)S(1)}, f32[1024,1024]{0,1:T(8,128)}, u32[]{:S(2)}) copy-start(f32[1024,1024]{0,1:T(8,128)} %copy-done) | copy-start | bytes 12582916
  159.0 3.4 %copy-start.2 = (f32[1024,1024]{0,1:T(8,128)S(1)}, f32[1024,1024]{0,1:T(8,128)}, u32[]{:S(2)}) copy-start(f32[1024,1024]{0,1:T(8,128)} %copy-done) | copy-start | bytes 12582916
  203.1 4.4 %copy-start.5 = (bf16[1024,512]{1,0:T(8,128)(2,1)S(1)}, bf16[1024,512]{1,0:T(8,128)(2,1)}, u32[]{:S(2)}) copy-start(bf16[1024,512]{1,0:T(8,128)(2,1)} %all-gather.2.cloned.1.call-done) | copy-start | bytes 3145732
  211.5 19.0 %all-to-all-start = ((bf16[16,16,1024]{2,1,0:T(8,128)(2,1)}), bf16[16,16,1024]{2,1,0:T(8,128)(2,1)S(1)}, u32[]{:S(2)}, u32[]{:S(2)}) async-start(bf16[16,16,1024]{2,1,0:T(8,128)(2,1)} %bitcast.4), calls=%async_computation | async-start | bytes 1048576 | tf_op jit(solution)/shard_map/all_to_all | solution.py:88
  219.2 29.7 %copy-start.3 = (bf16[32,256]{1,0:T(8,128)(2,1)S(1)}, bf16[32,256]{1,0:T(8,128)(2,1)}, u32[]{:S(2)}) copy-start(bf16[32,256]{1,0:T(8,128)(2,1)} %param.6) | copy-start | bytes 49156
  230.4 18.4 %all-to-all-start.1 = ((bf16[32,32,256]{2,1,0:T(8,128)(2,1)}), bf16[32,32,256]{2,1,0:T(8,128)(2,1)S(1)}, u32[]{:S(2)}, u32[]{:S(2)}) async-start(bf16[32,32,256]{2,1,0:T(8,128)(2,1)} %bitcast.6), calls=%async_computation.1 | async-start | bytes 1048576 | tf_op jit(solution)/shard_map/all_to_all | solution.py:81
Sparse Core Ops, SparseCore 0:
  11.4 56.3 all-gather.1
